TPU v7x, 32 devices: a whole 2x2x4 slice. The times are simulated.
32 devices in a mesh: member: 2 (over core), tile: 16 (over z, y, x).
Axes of the slice: x: 2, y: 2, z: 4, core: 2. Of those that a mesh axis runs over, the one named last changes fastest.
Arguments:
- member_predictions: bfloat16 [4, 80, 768, 1536], P(None, 'member', 'tile'), may hold values from -5 to 13
- meridional_operator: float32 [384, 128], replicated, may hold values from -0.3125 to 0.3125
- zonal_operator: float32 [256, 48], P('tile'), may hold values from -0.875 to 0.875
Outputs:
- coarse_anomalies: float32 [4, 80, 512, 256], P(None, None, 'tile', 'member')
All inputs are finite; a program needn't handle non-finite values.
Results may differ from a plain program's by a relative error of at most 0.0003.
Values sent between devices are 32-bit elements; how exact they have to be, the bound alone decides.
A program may use at most 128 MiB of HBM per device.

v0:
```python
import functools
import math

import jax
import jax.numpy as jnp
from jax import lax
from jax.experimental import pallas as pl
from jax.experimental.pallas import tpu as pltpu
from jax.sharding import PartitionSpec as P

MESH = pl.DeviceIdType.MESH
PACK = 8
DEPTH = 3


def two_parts(value):
    high = value.astype(jnp.bfloat16)
    low = (value - high.astype(jnp.float32)).astype(jnp.bfloat16)
    return high, low


def three_parts(value):
    high = value.astype(jnp.bfloat16)
    rest = value - high.astype(jnp.float32)
    middle = rest.astype(jnp.bfloat16)
    low = (rest - middle.astype(jnp.float32)).astype(jnp.bfloat16)
    return high, middle, low


def block_diagonal(part, width):
    coarse = part.shape[0]
    row = lax.broadcasted_iota(jnp.int32, (width, PACK * width), 0)
    col = lax.broadcasted_iota(jnp.int32, (width, PACK * width), 1)
    spread = col == row
    for f in range(1, PACK):
        spread = spread | (col == row + f * width)
    spread = jnp.where(spread, 1.0, 0.0).astype(jnp.bfloat16)
    wide = jnp.dot(part, spread, preferred_element_type=jnp.float32)
    tall = jnp.concatenate([wide] * PACK, axis=0)
    row = lax.broadcasted_iota(jnp.int32, tall.shape, 0)
    col = lax.broadcasted_iota(jnp.int32, tall.shape, 1)
    keep = None
    for f in range(PACK):
        here = (row >= f * coarse) & (row < (f + 1) * coarse) & (col >= f * width) & (col < (f + 1) * width)
        keep = here if keep is None else keep | here
    return jnp.where(keep, tall, 0.0).astype(jnp.bfloat16)


def exchange_kernel(
    members, tiles, x_ref, mer_ref, zon_ref, got_ref, xbuf, zon2, mer2, sendbuf, x_sem, send_sem, recv_sem, own_sem
):
    levels, local, width, fine = x_ref.shape
    block, per_block = mer_ref.shape
    groups, rows, lanes = sendbuf.shape[1:]
    per = PACK // levels
    spread = tiles // members
    half = tiles // 2
    me = lax.axis_index("member")
    tile = lax.axis_index("tile")
    target = tile // spread
    slot_there = me * spread + lax.rem(tile, spread)
    stays = target == me

    barrier = pltpu.get_barrier_semaphore()
    for h in range(members):
        for s in range(spread):
            source = me * spread + s

            @pl.when(jnp.logical_not((h == me) & (source == tile)))
            def _():
                pl.semaphore_signal(barrier, inc=1, device_id=(h, source), device_id_type=MESH)

    def fetch(g, slot):
        return pltpu.make_async_copy(x_ref.at[:, pl.ds(g * per, per)], xbuf.at[slot], x_sem.at[slot])

    for g in range(min(DEPTH, groups)):
        fetch(g, g).start()

    zon_high, zon_low = two_parts(zon_ref[...])
    zon2[: PACK * zon_ref.shape[0]] = block_diagonal(zon_high, width)
    zon2[PACK * zon_ref.shape[0] :] = block_diagonal(zon_low, width)
    mer_high, mer_low = two_parts(mer_ref[...].T)
    mer2[:per_block] = mer_high
    mer2[per_block:] = mer_low

    def destination(k):
        side = tile // half
        side = 1 - side if k < half else side
        return side * half + lax.rem(lax.rem(tile, half) + k, half)

    def remote(k, g):
        there = destination(k)
        return pltpu.make_async_remote_copy(
            src_ref=sendbuf.at[there, g],
            dst_ref=got_ref.at[slot_there, g],
            send_sem=send_sem.at[k],
            recv_sem=recv_sem.at[slot_there],
            device_id=(target, there),
            device_id_type=MESH,
        )

    def step(g, _):
        slot = lax.rem(g, DEPTH)
        fetch(g, slot).wait()
        fields = xbuf[slot].reshape(PACK * width, fine)
        across = jnp.dot(zon2[...], fields, preferred_element_type=jnp.float32)
        across = across[lanes:] + across[:lanes]
        for b in range(fine // block):
            high, middle, low = three_parts(across[:, b * block : (b + 1) * block])
            parts = jnp.concatenate([high, middle, low], axis=0)
            out = lax.dot_general(
                mer2[...], parts, (((1,), (1,)), ((), ())), preferred_element_type=jnp.float32
            )
            top, bottom = out[:per_block], out[per_block:]
            total = top[:, 2 * lanes :] + bottom[:, lanes : 2 * lanes]
            total = total + top[:, lanes : 2 * lanes] + bottom[:, :lanes]
            total = total + top[:, :lanes]
            for q in range(per_block // rows):
                sendbuf[b * (per_block // rows) + q, g] = total[q * rows : (q + 1) * rows]

        @pl.when(g + DEPTH < groups)
        def _():
            fetch(g + DEPTH, slot).start()

        @pl.when(g == 0)
        def _():
            pl.semaphore_wait(barrier, tiles - jnp.where(stays, 1, 0))

        for k in range(tiles):
            if k == half:

                @pl.when(stays)
                def _():
                    pltpu.make_async_copy(sendbuf.at[tile, g], got_ref.at[slot_there, g], own_sem).start()

                @pl.when(jnp.logical_not(stays))
                def _():
                    remote(k, g).start()

            else:
                remote(k, g).start()
        return 0

    lax.fori_loop(0, groups, step, 0)

    def whole(k, slot):
        return pltpu.make_async_remote_copy(
            src_ref=sendbuf.at[destination(k)],
            dst_ref=got_ref.at[slot],
            send_sem=send_sem.at[k],
            recv_sem=recv_sem.at[slot],
            device_id=(target, destination(k)),
            device_id_type=MESH,
        )

    for k in range(tiles):
        if k == half:

            @pl.when(stays)
            def _():
                pltpu.make_async_copy(sendbuf.at[tile], got_ref.at[slot_there], own_sem).wait()

            @pl.when(jnp.logical_not(stays))
            def _():
                whole(k, slot_there).wait_send()

        else:
            whole(k, slot_there).wait_send()
    for slot in range(tiles):

        @pl.when(jnp.logical_not(stays & (slot_there == slot)))
        def _():
            whole(0, slot).wait_recv()


def swap_pieces(blocks, piece):
    lanes = blocks[0].shape[-1]
    lane = lax.broadcasted_iota(jnp.int32, blocks[0].shape, blocks[0].ndim - 1)
    axis = blocks[0].ndim - 1
    blocks = list(blocks)
    d = PACK // 2
    while d >= 1:
        shift = d * piece
        upper = (lane & shift) != 0
        for s in range(PACK):
            if s & d:
                continue
            a, b = blocks[s], blocks[s + d]
            if 2 * shift == lanes:
                both = pltpu.roll(jnp.where(upper, a, b), shift, axis)
                blocks[s] = jnp.where(upper, both, a)
                blocks[s + d] = jnp.where(upper, b, both)
            else:
                blocks[s] = jnp.where(upper, pltpu.roll(b, shift, axis), a)
                blocks[s + d] = jnp.where(upper, b, pltpu.roll(a, lanes - shift, axis))
        d //= 2
    return blocks


def anomaly_kernel(members, tiles, got_ref, out_ref):
    levels, count, rows, _ = out_ref.shape
    groups = got_ref.shape[1]
    lanes = got_ref.shape[3]
    per = PACK // levels
    local = count // members
    spread = tiles // members
    scale = 1.0 / math.sqrt(count - 1)
    for side in range(spread // PACK):
        columns = slice(side * lanes, (side + 1) * lanes)
        sums = tuple(jnp.zeros((rows, lanes), jnp.float32) for _ in range(levels))
        for h in range(members):
            base = h * spread + side * PACK

            def gather(g, sums, base=base, h=h):
                fields = swap_pieces([got_ref[base + s, g] for s in range(PACK)], lanes // PACK)
                sums = list(sums)
                for f in range(PACK):
                    level, m = divmod(f, per)
                    out_ref[level, h * local + g * per + m, :, columns] = fields[f]
                    sums[level] = sums[level] + fields[f]
                return tuple(sums)

            sums = lax.fori_loop(0, groups, gather, sums, unroll=2)
        means = [total / count for total in sums]

        def center(m, _):
            for level in range(levels):
                out_ref[level, m, :, columns] = (out_ref[level, m, :, columns] - means[level]) * scale
            return 0

        lax.fori_loop(0, count, center, 0, unroll=4)


def body(members, tiles, x, meridional, zonal):
    levels, local, width, fine = x.shape
    block, per_block = meridional.shape
    coarse = zonal.shape[0]
    lanes = PACK * coarse
    groups = levels * local // PACK
    rows = fine // block * per_block // tiles
    spread = tiles // members
    assert PACK % levels == 0 and local % (PACK // levels) == 0 and spread % PACK == 0 and per_block % rows == 0
    vmem = pl.BlockSpec(memory_space=pltpu.VMEM)
    anywhere = pl.BlockSpec(memory_space=pl.ANY)
    got = pl.pallas_call(
        functools.partial(exchange_kernel, members, tiles),
        out_shape=jax.ShapeDtypeStruct((tiles, groups, rows, lanes), jnp.float32),
        in_specs=[anywhere, vmem, vmem],
        out_specs=anywhere,
        scratch_shapes=[
            pltpu.VMEM((DEPTH, levels, PACK // levels, width, fine), jnp.bfloat16),
            pltpu.VMEM((2 * lanes, PACK * width), jnp.bfloat16),
            pltpu.VMEM((2 * per_block, block), jnp.bfloat16),
            pltpu.VMEM((tiles, groups, rows, lanes), jnp.float32),
            pltpu.SemaphoreType.DMA((DEPTH,)),
            pltpu.SemaphoreType.DMA((tiles,)),
            pltpu.SemaphoreType.DMA((tiles,)),
            pltpu.SemaphoreType.DMA,
        ],
        compiler_params=pltpu.CompilerParams(
            collective_id=0, has_side_effects=True, vmem_limit_bytes=40 * 1024 * 1024
        ),
        name="restrict_exchange",
    )(x, meridional, zonal)
    height = 8 if rows % 8 == 0 else rows
    return pl.pallas_call(
        functools.partial(anomaly_kernel, members, tiles),
        grid=(rows // height,),
        out_shape=jax.ShapeDtypeStruct((levels, local * members, rows, spread * coarse), jnp.float32),
        in_specs=[pl.BlockSpec((tiles, groups, height, lanes), lambda i: (0, 0, i, 0))],
        out_specs=pl.BlockSpec((levels, local * members, height, spread * coarse), lambda i: (0, 0, i, 0)),
        compiler_params=pltpu.CompilerParams(vmem_limit_bytes=40 * 1024 * 1024),
        name="center_scale",
    )(got)


def solution(mesh):
    members, tiles = mesh.shape["member"], mesh.shape["tile"]
    return jax.shard_map(
        functools.partial(body, members, tiles),
        mesh=mesh,
        in_specs=(P(None, "member", "tile", None), P(), P("tile", None)),
        out_specs=P(None, None, "tile", "member"),
        check_vma=False,
    )
```

profile of v0, /device:TPU:1, one launch (start us, length us, event | category | flops | bytes accessed | tf_op | source)
XLA Modules:
  0.0 143.1 jit_solution(3642472405366956987)
XLA Ops:
  0.0 0.0 copy-start
  0.0 0.9 copy-done
  0.9 0.0 copy-start.1
  0.9 0.7 copy-done.1
  1.6 120.7 %restrict_exchange.1.got_ref = f32[16,20,32,128]{3,2,1,0:T(8,128)S(1)} custom-call(bf16[4,40,48,1536]{3,2,1,0:T(8,128)(2,1)} %x_ref.1, f32[384,128]{1,0:T(8,128)S(1)} %copy-done, f32[16,48]{1,0:T(8,128)S(1)} %copy-done.1), custom_call_target="tpu_custom_call" | custom-call | tf_op jit(solution)/shard_map/restrict_exchange/pallas_call | solution.py:245
  122.4 20.7 %center_scale.1 = f32[4,80,32,128]{3,2,1,0:T(8,128)} custom-call(f32[16,20,32,128]{3,2,1,0:T(8,128)S(1)} %restrict_exchange.1.got_ref), custom_call_target="tpu_custom_call" | custom-call | tf_op jit(solution)/shard_map/center_scale/pallas_call | solution.py:266
Async XLA Ops:
  0.0 0.9 copy-start
  0.9 0.7 copy-start.1
where the time goes:
time: 143 us
  Pallas kernels  141 us (99%)
  local copies, waits for them, and re-layouts  1.62 us (1%)
    pallas_call x1, Pallas kernels, body(): pl.pallas_call(functools.partial(exchange_kernel, members, tiles), out_sh...  121 us
    pallas_call x1, Pallas kernels, body(): pl.pallas_call(functools.partial(anomaly_kernel, members, tiles), grid=(r...  20.7 us

commit v1 on v0

v1 whole, which is shorter than its diff:
```python
import functools
import math

import jax
import jax.numpy as jnp
from jax import lax
from jax.experimental import pallas as pl
from jax.experimental.pallas import tpu as pltpu
from jax.sharding import PartitionSpec as P

MESH = pl.DeviceIdType.MESH
PACK = 8
DEPTH = 3


def two_parts(value):
    high = value.astype(jnp.bfloat16)
    low = (value - high.astype(jnp.float32)).astype(jnp.bfloat16)
    return high, low


def three_parts(value):
    high = value.astype(jnp.bfloat16)
    rest = value - high.astype(jnp.float32)
    middle = rest.astype(jnp.bfloat16)
    low = (rest - middle.astype(jnp.float32)).astype(jnp.bfloat16)
    return high, middle, low


def block_diagonal(part, width):
    coarse = part.shape[0]
    row = lax.broadcasted_iota(jnp.int32, (width, PACK * width), 0)
    col = lax.broadcasted_iota(jnp.int32, (width, PACK * width), 1)
    spread = col == row
    for f in range(1, PACK):
        spread = spread | (col == row + f * width)
    spread = jnp.where(spread, 1.0, 0.0).astype(jnp.bfloat16)
    wide = jnp.dot(part, spread, preferred_element_type=jnp.float32)
    tall = jnp.concatenate([wide] * PACK, axis=0)
    row = lax.broadcasted_iota(jnp.int32, tall.shape, 0)
    col = lax.broadcasted_iota(jnp.int32, tall.shape, 1)
    keep = None
    for f in range(PACK):
        here = (row >= f * coarse) & (row < (f + 1) * coarse) & (col >= f * width) & (col < (f + 1) * width)
        keep = here if keep is None else keep | here
    return jnp.where(keep, tall, 0.0).astype(jnp.bfloat16)


def swap_pieces(blocks, piece):
    lanes = blocks[0].shape[-1]
    lane = lax.broadcasted_iota(jnp.int32, blocks[0].shape, blocks[0].ndim - 1)
    axis = blocks[0].ndim - 1
    blocks = list(blocks)
    d = PACK // 2
    while d >= 1:
        shift = d * piece
        upper = (lane & shift) != 0
        for s in range(PACK):
            if s & d:
                continue
            a, b = blocks[s], blocks[s + d]
            if 2 * shift == lanes:
                both = pltpu.roll(jnp.where(upper, a, b), shift, axis)
                blocks[s] = jnp.where(upper, both, a)
                blocks[s + d] = jnp.where(upper, b, both)
            else:
                blocks[s] = jnp.where(upper, pltpu.roll(b, shift, axis), a)
                blocks[s + d] = jnp.where(upper, b, pltpu.roll(a, lanes - shift, axis))
        d //= 2
    return blocks


def exchange_kernel(
    members,
    tiles,
    x_ref,
    mer_hbm,
    zon_hbm,
    raw_ref,
    mean_ref,
    xbuf,
    mer_ref,
    zon_ref,
    zon2,
    mer2,
    sendbuf,
    got_ref,
    rawbuf,
    sumbuf,
    x_sem,
    op_sem,
    send_sem,
    recv_sem,
    own_sem,
    out_sem,
):
    levels, local, width, fine = x_ref.shape
    block, per_block = mer_ref.shape
    groups, rows, lanes = sendbuf.shape[1:]
    per = PACK // levels
    spread = tiles // members
    half = tiles // 2
    me = lax.axis_index("member")
    tile = lax.axis_index("tile")
    target = tile // spread
    slot_there = me * spread + lax.rem(tile, spread)
    stays = target == me

    barrier = pltpu.get_barrier_semaphore()
    for h in range(members):
        for s in range(spread):
            source = me * spread + s

            @pl.when(jnp.logical_not((h == me) & (source == tile)))
            def _():
                pl.semaphore_signal(barrier, inc=1, device_id=(h, source), device_id_type=MESH)

    def fetch(g, slot):
        return pltpu.make_async_copy(x_ref.at[:, pl.ds(g * per, per)], xbuf.at[slot], x_sem.at[slot])

    operators = [
        pltpu.make_async_copy(zon_hbm, zon_ref, op_sem.at[0]),
        pltpu.make_async_copy(mer_hbm, mer_ref, op_sem.at[1]),
    ]
    for copy in operators:
        copy.start()
    for g in range(min(DEPTH, groups)):
        fetch(g, g).start()
    for copy in operators:
        copy.wait()

    zon_high, zon_low = two_parts(zon_ref[...])
    zon2[: PACK * zon_ref.shape[0]] = block_diagonal(zon_high, width)
    zon2[PACK * zon_ref.shape[0] :] = block_diagonal(zon_low, width)
    mer_high, mer_low = two_parts(mer_ref[...].T)
    mer2[:per_block] = mer_high
    mer2[per_block:] = mer_low

    def destination(k):
        side = tile // half
        side = 1 - side if k < half else side
        return side * half + lax.rem(lax.rem(tile, half) + k, half)

    def remote(k, g):
        there = destination(k)
        return pltpu.make_async_remote_copy(
            src_ref=sendbuf.at[there, g],
            dst_ref=got_ref.at[slot_there, g],
            send_sem=send_sem.at[k],
            recv_sem=recv_sem.at[slot_there, g],
            device_id=(target, there),
            device_id_type=MESH,
        )

    def step(g, _):
        slot = lax.rem(g, DEPTH)
        fetch(g, slot).wait()
        fields = xbuf[slot].reshape(PACK * width, fine)
        across = jnp.dot(zon2[...], fields, preferred_element_type=jnp.float32)
        across = across[lanes:] + across[:lanes]
        for b in range(fine // block):
            high, middle, low = three_parts(across[:, b * block : (b + 1) * block])
            parts = jnp.concatenate([high, middle, low], axis=0)
            out = lax.dot_general(
                mer2[...], parts, (((1,), (1,)), ((), ())), preferred_element_type=jnp.float32
            )
            top, bottom = out[:per_block], out[per_block:]
            total = top[:, 2 * lanes :] + bottom[:, lanes : 2 * lanes]
            total = total + top[:, lanes : 2 * lanes] + bottom[:, :lanes]
            total = total + top[:, :lanes]
            for q in range(per_block // rows):
                sendbuf[b * (per_block // rows) + q, g] = total[q * rows : (q + 1) * rows]

        @pl.when(g + DEPTH < groups)
        def _():
            fetch(g + DEPTH, slot).start()

        @pl.when(g == 0)
        def _():
            pl.semaphore_wait(barrier, tiles - jnp.where(stays, 1, 0))

        for k in range(tiles):
            if k == half:

                @pl.when(stays)
                def _():
                    pltpu.make_async_copy(sendbuf.at[tile, g], got_ref.at[slot_there, g], own_sem).start()

                @pl.when(jnp.logical_not(stays))
                def _():
                    remote(k, g).start()

            else:
                remote(k, g).start()
        return 0

    lax.fori_loop(0, groups, step, 0)

    @pl.when(stays)
    def _():
        pltpu.make_async_copy(sendbuf.at[tile], got_ref.at[slot_there], own_sem).wait()

    sumbuf[...] = jnp.zeros_like(sumbuf)
    count = members * local

    def arrival(g, _):
        for slot in range(tiles):

            @pl.when(jnp.logical_not(stays & (slot_there == slot)))
            def _():
                pltpu.make_async_remote_copy(
                    src_ref=sendbuf.at[0, g],
                    dst_ref=got_ref.at[slot, g],
                    send_sem=send_sem.at[0],
                    recv_sem=recv_sem.at[slot, g],
                    device_id=(target, destination(0)),
                    device_id_type=MESH,
                ).wait_recv()

        for h in range(members):
            for side in range(spread // PACK):
                base = h * spread + side * PACK
                columns = slice(side * lanes, (side + 1) * lanes)
                fields = swap_pieces([got_ref[base + s, g] for s in range(PACK)], lanes // PACK)
                for f in range(PACK):
                    rawbuf[f // per, h * local + g * per + f % per, :, columns] = fields[f]
                for level in range(levels):
                    total = fields[level * per]
                    for m in range(1, per):
                        total = total + fields[level * per + m]
                    sumbuf[level, :, columns] += total
            done = pl.ds(h * local + g * per, per)
            pltpu.make_async_copy(rawbuf.at[:, done], raw_ref.at[:, done], out_sem.at[0]).start()
        return 0

    lax.fori_loop(0, groups, arrival, 0)
    sumbuf[...] = sumbuf[...] / count
    mean = pltpu.make_async_copy(sumbuf, mean_ref, out_sem.at[1])
    mean.start()

    def whole(k):
        return pltpu.make_async_remote_copy(
            src_ref=sendbuf.at[destination(k)],
            dst_ref=got_ref.at[slot_there],
            send_sem=send_sem.at[k],
            recv_sem=recv_sem.at[slot_there, 0],
            device_id=(target, destination(k)),
            device_id_type=MESH,
        )

    for k in range(tiles):
        if k == half:

            @pl.when(jnp.logical_not(stays))
            def _():
                whole(k).wait_send()

        else:
            whole(k).wait_send()
    pltpu.make_async_copy(rawbuf, raw_ref, out_sem.at[0]).wait()
    mean.wait()


def body(members, tiles, x, meridional, zonal):
    levels, local, width, fine = x.shape
    block, per_block = meridional.shape
    coarse = zonal.shape[0]
    lanes = PACK * coarse
    groups = levels * local // PACK
    rows = fine // block * per_block // tiles
    spread = tiles // members
    assert PACK % levels == 0 and local % (PACK // levels) == 0 and spread % PACK == 0 and per_block % rows == 0
    anywhere = pl.BlockSpec(memory_space=pl.ANY)
    count = local * members
    columns = spread * coarse
    raw, mean = pl.pallas_call(
        functools.partial(exchange_kernel, members, tiles),
        out_shape=[
            jax.ShapeDtypeStruct((levels, count, rows, columns), jnp.float32),
            jax.ShapeDtypeStruct((levels, rows, columns), jnp.float32),
        ],
        in_specs=[pl.BlockSpec(memory_space=pltpu.HBM)] * 3,
        out_specs=[anywhere] * 2,
        scratch_shapes=[
            pltpu.VMEM((DEPTH, levels, PACK // levels, width, fine), jnp.bfloat16),
            pltpu.VMEM(meridional.shape, jnp.float32),
            pltpu.VMEM(zonal.shape, jnp.float32),
            pltpu.VMEM((2 * lanes, PACK * width), jnp.bfloat16),
            pltpu.VMEM((2 * per_block, block), jnp.bfloat16),
            pltpu.VMEM((tiles, groups, rows, lanes), jnp.float32),
            pltpu.VMEM((tiles, groups, rows, lanes), jnp.float32),
            pltpu.VMEM((levels, count, rows, columns), jnp.float32),
            pltpu.VMEM((levels, rows, columns), jnp.float32),
            pltpu.SemaphoreType.DMA((DEPTH,)),
            pltpu.SemaphoreType.DMA((2,)),
            pltpu.SemaphoreType.DMA((tiles,)),
            pltpu.SemaphoreType.DMA((tiles, groups)),
            pltpu.SemaphoreType.DMA,
            pltpu.SemaphoreType.DMA((2,)),
        ],
        compiler_params=pltpu.CompilerParams(
            collective_id=0, has_side_effects=True, vmem_limit_bytes=40 * 1024 * 1024
        ),
        name="restrict_exchange",
    )(x, meridional, zonal)
    return (raw - mean[:, None]) * (1.0 / math.sqrt(count - 1))


def solution(mesh):
    members, tiles = mesh.shape["member"], mesh.shape["tile"]
    return jax.shard_map(
        functools.partial(body, members, tiles),
        mesh=mesh,
        in_specs=(P(None, "member", "tile", None), P(), P("tile", None)),
        out_specs=P(None, None, "tile", "member"),
        check_vma=False,
    )
```

time: 143 us -> 129 us (0.902)
  Pallas kernels: 141 us -> 124 us
  other arithmetic: 0 us -> 3.04 us
    pallas_call x1 -> x0, Pallas kernels: 20.7 us -> none  [body(): pl.pallas_call(functools.partial(anomaly_kernel, members, tiles), grid=(r...]
    pallas_call x1, Pallas kernels: 121 us -> 124 us  [body(): pl.pallas_call(functools.partial(exchange_kernel, members, tiles), out_sh...]
    mul x0 -> x1, other arithmetic: none -> 3.04 us  [body(): return (raw - mean[:, None]) * (1.0 / math.sqrt(count - 1))]
where the time goes in v1:
time: 129 us
  Pallas kernels  124 us (96%)
  other arithmetic  3.04 us (2%)
  local copies, waits for them, and re-layouts  1.62 us (1%)
    pallas_call x1, Pallas kernels, body(): pl.pallas_call(functools.partial(exchange_kernel, members, tiles), out_sh...  124 us
    mul x1, other arithmetic, body(): return (raw - mean[:, None]) * (1.0 / math.sqrt(count - 1))  3.04 us

profile of v1, /device:TPU:1, one launch (start us, length us, event | category | flops | bytes accessed | tf_op | source)
XLA Modules:
  0.0 129.1 jit_solution(615646905091048410)
XLA Ops:
  0.0 0.0 copy-start
  0.0 0.9 copy-done
  0.9 0.0 copy-start.1
  0.9 0.7 copy-done.1
  1.6 124.4 %restrict_exchange.1 = (f32[4,80,32,128]{3,2,1,0:T(8,128)S(1)}, f32[4,32,128]{2,1,0:T(8,128)S(1)}) custom-call(bf16[4,40,48,1536]{3,2,1,0:T(8,128)(2,1)} %x_ref.1, f32[384,128]{1,0:T(8,128)S(1)} %copy-done, f32[16,48]{1,0:T(8,128)S(1)} %copy-done.1), custom_call_target="tpu_custom_call" | custom-call | tf_op jit(solution)/shard_map/restrict_exchange/pallas_call | solution.py:276
  126.1 3.0 %subtract_multiply_fusion = f32[4,80,32,128]{3,2,1,0:T(8,128)} fusion(f32[4,80,32,128]{3,2,1,0:T(8,128)S(1)} %get-tuple-element.7, f32[4,32,128]{2,1,0:T(8,128)S(1)} %get-tuple-element.8), kind=kLoop, calls=%fused_computation | loop fusion | flops 2621440 | bytes 10551296 | tf_op jit(solution)/shard_map/mul | solution.py:306
Async XLA Ops:
  0.0 0.9 copy-start
  0.9 0.7 copy-start.1
